TPU v7x, 512 devices: a whole 4x8x8 slice. The times are simulated.
512 devices in a mesh: row: 32 (over z, y_hi, core), col: 16 (over y_lo, x).
Axes of the slice: x: 4, y: 8 (y_hi: 2, y_lo: 4; y = y_hi * 4 + y_lo), z: 8, core: 2. Of those that a mesh axis runs over, the one named last changes fastest.
Arguments:
- upper: bfloat16 [16384, 32768], P('col', 'row'), may hold values from -6 to 6
- lower: bfloat16 [32768, 16384], P('col', 'row'), may hold values from -0.15625 to 0.15625
- upper_tiles: int32 [128, 256], P('col', 'row'), may hold values from 0 to 1, as said below
- lower_tiles: int32 [256, 128], P('col', 'row'), may hold values from 0 to 1, as said below
Outputs:
- enlarged: bfloat16 [16384, 16384], P('col', 'row')
Inputs may be any that keep to these rules, and one draw needn't show every extreme that they name: `upper_tiles`: a tile is 1 exactly where the charge of its row tile equals the charge of its contracted tile (upper) or the charge of its contracted tile equals that of its column tile (lower), charges 0, 1 or 2, laid out in the stored rotated order; both halves share the contracted tiles' charges. `lower_tiles`: charge occupancy of the lower half as described for upper_tiles.
All inputs are finite; a program needn't handle non-finite values.
Results may differ from a plain program's by a relative error of at most 0.001.
Values may be sent and summed in bfloat16 or wider, within the bound.
A program may use at most 64 MiB of HBM per device.

v0:
```python
import jax
import jax.numpy as jnp
from jax import lax
from jax.sharding import PartitionSpec as P

STEPS = 4


def shifted(value, axis, by):
    length = lax.axis_size(axis)
    return lax.ppermute(value, axis, [(i, (i + by) % length) for i in range(length)])


def apply_tiles(values, tiles, tile_size):
    rows, cols = values.shape
    shaped = values.reshape(rows // tile_size, tile_size, cols // tile_size, tile_size)
    masked = shaped * tiles.astype(values.dtype)[:, None, :, None]
    return masked.reshape(rows, cols)


def body(upper, lower, upper_tiles, lower_tiles):
    tile_size = upper.shape[0] // upper_tiles.shape[0]
    masked_upper = apply_tiles(upper, upper_tiles, tile_size)
    masked_lower = apply_tiles(lower, lower_tiles, tile_size)
    block = masked_upper.shape[1]
    ratio = masked_lower.shape[0] // block
    upper_blocks = [masked_upper]
    current = masked_upper
    for step_index in range(1, STEPS):
        current = shifted(current, "row", -1)
        upper_blocks.append(current)
    lower_held = masked_lower
    accumulated = jnp.zeros((masked_upper.shape[0], masked_lower.shape[1]), jnp.float32)
    for step_index in range(STEPS):
        if step_index > 0 and step_index % ratio == 0:
            lower_held = shifted(lower_held, "col", -1)
        offset = step_index % ratio * block
        lower_rows = lower_held[offset : offset + block]
        accumulated = accumulated + jnp.dot(
            upper_blocks[step_index], lower_rows, preferred_element_type=jnp.float32
        )
    return accumulated.astype(jnp.bfloat16)


def solution(mesh):
    in_specs = (P("col", "row"), P("col", "row"), P("col", "row"), P("col", "row"))
    out_specs = P("col", "row")
    return jax.shard_map(body, mesh=mesh, in_specs=in_specs, out_specs=out_specs, check_vma=False)
```

profile of v0, /device:TPU:14, one launch (start us, length us, event | category | flops | bytes accessed | tf_op | source)
XLA Modules:
  0.0 215.2 jit_solution(2559183216738334737)
XLA Ops:
  0.0 0.8 convert_element_type.9
  0.8 0.3 mul.24
  1.2 0.4 copy-done.1
  1.6 0.3 bitcast_multiply_fusion.1
  1.9 1.3 copy-done.2
  3.2 14.9 %collective-permute-start = (bf16[1024,1024]{1,0:T(8,128)(2,1)S(1)}, bf16[1024,1024]{1,0:T(8,128)(2,1)}, u32[]{:S(2)}, u32[]{:S(2)}) collective-permute-start(bf16[1024,1024]{1,0:T(8,128)(2,1)S(1)} %bitcast_multiply_fusion.1), channel_id=1, source_target_pairs={{0,496},{16,0},{32,16},{48,32},{64,48},{80,64},{96,80},{112,96},{1... | collective-permute-start | bytes 6291464 | tf_op jit(solution)/shard_map/ppermute | solution.py:11
  18.1 46.0 %collective-permute-done = bf16[1024,1024]{1,0:T(8,128)(2,1)} collective-permute-done((bf16[1024,1024]{1,0:T(8,128)(2,1)S(1)}, bf16[1024,1024]{1,0:T(8,128)(2,1)}, u32[]{:S(2)}, u32[]{:S(2)}) %collective-permute-start) | collective-permute-done | bytes 2097184 | tf_op jit(solution)/shard_map/ppermute | solution.py:11
  64.1 10.1 %collective-permute-start.1 = (bf16[1024,1024]{1,0:T(8,128)(2,1)}, bf16[1024,1024]{1,0:T(8,128)(2,1)}, u32[]{:S(2)}, u32[]{:S(2)}) collective-permute-start(bf16[1024,1024]{1,0:T(8,128)(2,1)} %collective-permute-done), channel_id=1, source_target_pairs={{0,496},{16,0},{32,16},{48,32},{64,48},{80,64},{96,80},{112,96},{1... | collective-permute-start | bytes 6291464 | tf_op jit(solution)/shard_map/ppermute | solution.py:11
  74.3 0.1 copy.5
  74.4 0.6 mul.27
  75.0 1.6 bitcast_multiply_fusion
  76.6 2.7 %collective-permute-start.2 = (bf16[2048,512]{1,0:T(8,128)(2,1)}, bf16[2048,512]{1,0:T(8,128)(2,1)}, u32[]{:S(2)}, u32[]{:S(2)}) collective-permute-start(bf16[2048,512]{1,0:T(8,128)(2,1)} %bitcast_multiply_fusion), channel_id=1, source_target_pairs={{0,15},{1,0},{2,1},{3,2},{4,3},{5,4},{6,5},{7,6},{8,7},{9,8},{10,9... | collective-permute-start | bytes 6291464 | tf_op jit(solution)/shard_map/ppermute | solution.py:11
  79.3 39.3 %collective-permute-done.1 = bf16[1024,1024]{1,0:T(8,128)(2,1)} collective-permute-done((bf16[1024,1024]{1,0:T(8,128)(2,1)}, bf16[1024,1024]{1,0:T(8,128)(2,1)}, u32[]{:S(2)}, u32[]{:S(2)}) %collective-permute-start.1) | collective-permute-done | bytes 2097184 | tf_op jit(solution)/shard_map/ppermute | solution.py:11
  118.7 10.0 %collective-permute-start.3 = (bf16[1024,1024]{1,0:T(8,128)(2,1)}, bf16[1024,1024]{1,0:T(8,128)(2,1)}, u32[]{:S(2)}, u32[]{:S(2)}) collective-permute-start(bf16[1024,1024]{1,0:T(8,128)(2,1)} %collective-permute-done.1), channel_id=1, source_target_pairs={{0,496},{16,0},{32,16},{48,32},{64,48},{80,64},{96,80},{112,96},{1... | collective-permute-start | bytes 6291464 | tf_op jit(solution)/shard_map/ppermute | solution.py:11
  128.7 2.1 reshape.12
  130.8 2.6 %broadcast_multiply_fusion = bf16[16,128,4,128]{3,2,1,0:T(4,128)(2,1)S(1)} fusion(bf16[16,128,4,128]{3,2,1,0:T(4,128)(2,1)} %reshape.12, bf16[16,4]{1,0:T(8,128)(2,1)S(1)} %copy.5), kind=kLoop, calls=%fused_computation.12 | loop fusion | flops 1048576 | bytes 4194432 | tf_op jit(solution)/shard_map/mul | solution.py:17
  133.3 0.8 fusion.9
  134.1 0.8 copy-done.3
  134.9 1.3 fusion.3
  136.2 2.8 %fusion = f32[1024,512]{1,0:T(8,128)S(1)} fusion(bf16[1024,1024]{1,0:T(8,128)(2,1)} %collective-permute-done, bf16[128,8,4,128]{3,2,1,0:T(4,128)(2,1)S(1)} %bitcast.24), kind=kOutput, calls=%fused_computation.3 | convolution fusion | flops 1073741824 | bytes 5242880 | tf_op jit(solution)/shard_map/dot_general | solution.py:39
  139.0 68.9 %collective-permute-done.2 = bf16[2048,512]{1,0:T(8,128)(2,1)} collective-permute-done((bf16[2048,512]{1,0:T(8,128)(2,1)}, bf16[2048,512]{1,0:T(8,128)(2,1)}, u32[]{:S(2)}, u32[]{:S(2)}) %collective-permute-start.2) | collective-permute-done | bytes 2097184 | tf_op jit(solution)/shard_map/ppermute | solution.py:11
  207.9 3.1 %fusion.7 = f32[1024,512]{1,0:T(8,128)S(1)} fusion(bf16[1024,1024]{1,0:T(8,128)(2,1)} %collective-permute-done.1, bf16[2048,512]{1,0:T(8,128)(2,1)} %collective-permute-done.2), kind=kOutput, calls=%fused_computation.10 | convolution fusion | flops 1073741824 | bytes 5242880 | tf_op jit(solution)/shard_map/dot_general | solution.py:39
  211.0 0.0 collective-permute-done.3
  211.0 4.1 %add_convert_fusion = bf16[1024,512]{1,0:T(8,128)(2,1)} fusion(f32[1024,512]{1,0:T(8,128)S(1)} %fusion.7, f32[1024,512]{1,0:T(8,128)S(1)} %fusion.3, f32[1024,512]{1,0:T(8,128)S(1)} %fusion, bf16[1024,1024]{1,0:T(8,128)(2,1)} %collective-permute-done.3, bf16[2048,512]{1,0:T(8,128)(2,1)} %collective-permute-done.2), kind=kOutput, calls=%fused_computation.2 | convolution fusion | flops 1075838976 | bytes 10485760 | tf_op jit(solution)/shard_map/dot_general | solution.py:39
  (8 shorter events, 0.0 us)
Async XLA Ops:
  0.0 1.6 copy-start.1
  1.6 72.6 %copy-start.4 = (s32[16,4]{0,1:T(4,128)S(1)}, s32[16,4]{0,1:T(4,128)}, u32[]{:S(2)}) copy-start(s32[16,4]{0,1:T(4,128)} %param.7) | copy-start | bytes 772
  1.9 1.4 copy-start.2
  3.2 71.7 %copy-start = (bf16[2048,512]{1,0:T(8,128)(2,1)S(1)}, bf16[2048,512]{1,0:T(8,128)(2,1)}, u32[]{:S(2)}) copy-start(bf16[2048,512]{1,0:T(8,128)(2,1)} %param.5) | copy-start | bytes 6291460
  3.2 60.9 %collective-permute-start = (bf16[1024,1024]{1,0:T(8,128)(2,1)S(1)}, bf16[1024,1024]{1,0:T(8,128)(2,1)}, u32[]{:S(2)}, u32[]{:S(2)}) collective-permute-start(bf16[1024,1024]{1,0:T(8,128)(2,1)S(1)} %bitcast_multiply_fusion.1), channel_id=1, source_target_pairs={{0,496},{16,0},{32,16},{48,32},{64,48},{80,64},{96,80},{112,96},{1... | collective-permute-start | bytes 6291464 | tf_op jit(solution)/shard_map/ppermute | solution.py:11
  64.1 54.5 %collective-permute-start.1 = (bf16[1024,1024]{1,0:T(8,128)(2,1)}, bf16[1024,1024]{1,0:T(8,128)(2,1)}, u32[]{:S(2)}, u32[]{:S(2)}) collective-permute-start(bf16[1024,1024]{1,0:T(8,128)(2,1)} %collective-permute-done), channel_id=1, source_target_pairs={{0,496},{16,0},{32,16},{48,32},{64,48},{80,64},{96,80},{112,96},{1... | collective-permute-start | bytes 6291464 | tf_op jit(solution)/shard_map/ppermute | solution.py:11
  76.6 131.3 %collective-permute-start.2 = (bf16[2048,512]{1,0:T(8,128)(2,1)}, bf16[2048,512]{1,0:T(8,128)(2,1)}, u32[]{:S(2)}, u32[]{:S(2)}) collective-permute-start(bf16[2048,512]{1,0:T(8,128)(2,1)} %bitcast_multiply_fusion), channel_id=1, source_target_pairs={{0,15},{1,0},{2,1},{3,2},{4,3},{5,4},{6,5},{7,6},{8,7},{9,8},{10,9... | collective-permute-start | bytes 6291464 | tf_op jit(solution)/shard_map/ppermute | solution.py:11
  118.7 92.4 %collective-permute-start.3 = (bf16[1024,1024]{1,0:T(8,128)(2,1)}, bf16[1024,1024]{1,0:T(8,128)(2,1)}, u32[]{:S(2)}, u32[]{:S(2)}) collective-permute-start(bf16[1024,1024]{1,0:T(8,128)(2,1)} %collective-permute-done.1), channel_id=1, source_target_pairs={{0,496},{16,0},{32,16},{48,32},{64,48},{80,64},{96,80},{112,96},{1... | collective-permute-start | bytes 6291464 | tf_op jit(solution)/shard_map/ppermute | solution.py:11
  133.3 1.6 copy-start.3
where the time goes:
time: 216 us; the launch traced here: 215 us
  waiting for transfers between devices  154 us (71%)
  starting transfers between devices  37.7 us (17%)
  matrix products  11.3 us (5%)
  local copies, waits for them, and re-layouts  6.48 us (3%)
  other arithmetic  5.29 us (2%)
    ppermute x4, waiting for transfers between devices, shifted(): lax.ppermute(value, axis, [(i, (i + by) % length) for i in range(length)])  154 us
    ppermute x4, starting transfers between devices, shifted(): lax.ppermute(value, axis, [(i, (i + by) % length) for i in range(length)])  37.7 us
    dot_general x4, matrix products, body(): jnp.dot(upper_blocks[step_index], lower_rows, preferred_element_type=jnp....  11.3 us
    mul x3, other arithmetic, apply_tiles(): masked = shaped * tiles.astype(values.dtype)[:, None, :, None]  4.44 us
  transfers between devices with their start and end apart: 4, of which 3 were waited for; matrix products, arithmetic and copies ran while one was open for 7% of the time, Pallas kernels for 0%

commit v1 on v0

v1 whole, which is shorter than its diff:
```python
import jax
import jax.numpy as jnp
from jax import lax
from jax.experimental import pallas as pl
from jax.experimental.pallas import tpu as pltpu
from jax.sharding import PartitionSpec as P

STEPS = 4
TILE = 128
X = 4
PARTS = 4
MESH = pl.DeviceIdType.MESH


def kernel(
    n_row, n_col, upper_tiles, lower_tiles, upper, lower, out,
    ublocks, lblocks, relay, result,
    uload, lload, near_send, near_recv, far_send, far_recv, pair_send, pair_recv,
    low_send, low_recv, hop_send, hop_recv, store_sem,
):
    r, c = lax.axis_index("row"), lax.axis_index("col")
    core, x = r % 2, c % X
    even = core == 0
    rows = TILE
    chunks = upper.shape[0] // rows
    held = lower.shape[0]
    quarter = held // PARTS

    def dev(dr, dc):
        return (lax.rem(r + dr + n_row, n_row), lax.rem(c + dc + n_col, n_col))

    first = x == 0
    last = x == X - 1
    origin_c = c - x
    goal = (r, lax.rem(origin_c + n_col - 1, n_col))

    barrier = pltpu.get_barrier_semaphore()

    def greet(device):
        pl.semaphore_signal(barrier, inc=1, device_id=device, device_id_type=MESH)

    for i in range(chunks):
        pltpu.make_async_copy(
            upper.at[pl.ds(i * rows, rows)], ublocks.at[0, pl.ds(i * rows, rows)], uload.at[i]
        ).start()
    for i in range(PARTS):
        pltpu.make_async_copy(
            lower.at[pl.ds(i * quarter, quarter)], lblocks.at[pl.ds(i * quarter, quarter)], lload.at[i]
        ).start()

    greet(dev(2, 0))
    greet(dev(jnp.where(even, 1, 3), 0))
    greet(dev(jnp.where(even, 1, -1), 0))

    @pl.when(jnp.logical_not(last))
    def _():
        greet(dev(0, 1))

    @pl.when(last)
    def _():
        for j in range(PARTS):
            greet((r, lax.rem(origin_c + X + j, n_col)))

    @pl.when(jnp.logical_not(first))
    def _():
        greet((r, origin_c))

    pl.semaphore_wait(barrier, jnp.where(first, 3 + 1 + 3, 3 + 1 + 1))

    def near(i):
        part = pl.ds(pl.multiple_of(i * rows, rows), rows)
        return pltpu.make_async_remote_copy(
            ublocks.at[0, part], ublocks.at[2, part], near_send.at[i], near_recv.at[i],
            device_id=dev(-2, 0), device_id_type=MESH,
        )

    def far(i):
        part = pl.ds(pl.multiple_of(i * rows, rows), rows)
        return pltpu.make_async_remote_copy(
            ublocks.at[0, part], ublocks.at[jnp.where(even, 3, 1), part], far_send.at[i], far_recv.at[i],
            device_id=dev(jnp.where(even, -3, -1), 0), device_id_type=MESH,
        )

    def pair(i):
        part = pl.ds(pl.multiple_of(i * rows, rows), rows)
        return pltpu.make_async_remote_copy(
            ublocks.at[2, part], ublocks.at[jnp.where(even, 1, 3), part], pair_send.at[i], pair_recv.at[i],
            device_id=dev(jnp.where(even, 1, -1), 0), device_id_type=MESH,
        )

    def low(j):
        return pltpu.make_async_remote_copy(
            lblocks.at[pl.ds(j * quarter, quarter)], lblocks.at[pl.ds(held + j * quarter, quarter)],
            low_send.at[j], low_recv.at[j], device_id=dev(0, -1), device_id_type=MESH,
        )

    def hop(j):
        return pltpu.make_async_remote_copy(
            lblocks.at[pl.ds(j * quarter, quarter)], relay, hop_send.at[j], hop_recv.at[0],
            device_id=(r, lax.rem(origin_c + j, n_col)), device_id_type=MESH,
        )

    def goal_first():
        return pltpu.make_async_remote_copy(
            lblocks.at[pl.ds(0, quarter)], lblocks.at[pl.ds(held, quarter)],
            low_send.at[0], low_recv.at[0], device_id=goal, device_id_type=MESH,
        )

    def goal_relay():
        return pltpu.make_async_remote_copy(
            relay, lblocks.at[pl.ds(pl.multiple_of(held + x * quarter, quarter), quarter)],
            hop_send.at[0], low_recv.at[x], device_id=goal, device_id_type=MESH,
        )

    def mask_upper(i):
        part = pl.ds(pl.multiple_of(i * rows, rows), rows)
        for k in range(upper.shape[1] // TILE):
            at = (0, part, pl.ds(k * TILE, TILE))
            keep = upper_tiles[i, k].astype(jnp.float32)
            ublocks[at] = ublocks[at] * jnp.full((rows, TILE), keep, jnp.float32).astype(jnp.bfloat16)

    def mask_lower(i):
        part = pl.ds(pl.multiple_of(i * TILE, TILE), TILE)
        for k in range(lower.shape[1] // TILE):
            at = (part, pl.ds(k * TILE, TILE))
            keep = lower_tiles[i, k].astype(jnp.float32)
            lblocks[at] = lblocks[at] * jnp.full((TILE, TILE), keep, jnp.float32).astype(jnp.bfloat16)

    @pl.loop(0, chunks)
    def _(i):
        part = pl.ds(pl.multiple_of(i * rows, rows), rows)
        pltpu.make_async_copy(upper.at[part], ublocks.at[0, part], uload.at[i]).wait()
        mask_upper(i)
        near(i).start()
        far(i).start()

    for i in range(PARTS):
        pltpu.make_async_copy(
            lower.at[pl.ds(i * quarter, quarter)], lblocks.at[pl.ds(i * quarter, quarter)], lload.at[i]
        ).wait()

    @pl.loop(0, held // TILE)
    def _(i):
        mask_lower(i)

    @pl.when(first)
    def _():
        for j in range(1, PARTS):
            hop(j).start()
        goal_first().start()

    @pl.when(jnp.logical_not(first))
    def _():
        for j in range(PARTS):
            low(j).start()
        hop(1).wait_recv()
        goal_relay().start()

    def multiply(i):
        part = pl.ds(pl.multiple_of(i * rows, rows), rows)
        block = ublocks.shape[2]
        total = jnp.zeros((rows, lower.shape[1]), jnp.float32)
        for s in range(STEPS):
            total += jnp.dot(
                ublocks[s, part], lblocks[pl.ds(s * block, block)], preferred_element_type=jnp.float32
            )
        result[part] = total.astype(jnp.bfloat16)
        pltpu.make_async_copy(result.at[part], out.at[part], store_sem.at[i]).start()

    near(0).wait_recv()
    pair(0).start()
    for j in range(PARTS):
        low(j).wait_recv()

    @pl.loop(1, chunks)
    def _(i):
        near(i).wait_recv()
        pair(i).start()
        pair(i - 1).wait_recv()
        far(i - 1).wait_recv()
        multiply(i - 1)

    pair(chunks - 1).wait_recv()
    far(chunks - 1).wait_recv()
    multiply(chunks - 1)

    @pl.loop(0, chunks)
    def _(i):
        part = pl.ds(pl.multiple_of(i * rows, rows), rows)
        near(i).wait_send()
        far(i).wait_send()
        pair(i).wait_send()
        pltpu.make_async_copy(result.at[part], out.at[part], store_sem.at[i]).wait()

    @pl.when(first)
    def _():
        for j in range(1, PARTS):
            hop(j).wait_send()
        goal_first().wait_send()

    @pl.when(jnp.logical_not(first))
    def _():
        for j in range(PARTS):
            low(j).wait_send()
        goal_relay().wait_send()


def body(upper, lower, upper_tiles, lower_tiles):
    n_row, n_col = lax.axis_size("row"), lax.axis_size("col")
    rows, block = upper.shape
    held, cols = lower.shape
    chunks = rows // TILE
    dma = pltpu.SemaphoreType.DMA

    def run(*refs):
        kernel(n_row, n_col, *refs)

    return pl.pallas_call(
        run,
        out_shape=jax.ShapeDtypeStruct((rows, cols), jnp.bfloat16),
        in_specs=[pl.BlockSpec(memory_space=pltpu.SMEM)] * 2 + [pl.BlockSpec(memory_space=pl.ANY)] * 2,
        out_specs=pl.BlockSpec(memory_space=pl.ANY),
        scratch_shapes=[
            pltpu.VMEM((STEPS, rows, block), jnp.bfloat16),
            pltpu.VMEM((2 * held, cols), jnp.bfloat16),
            pltpu.VMEM((held // PARTS, cols), jnp.bfloat16),
            pltpu.VMEM((rows, cols), jnp.bfloat16),
            dma((chunks,)), dma((PARTS,)),
            dma((chunks,)), dma((chunks,)),
            dma((chunks,)), dma((chunks,)),
            dma((chunks,)), dma((chunks,)),
            dma((PARTS,)), dma((PARTS,)),
            dma((PARTS,)), dma((1,)),
            dma((chunks,)),
        ],
        compiler_params=pltpu.CompilerParams(
            collective_id=0, has_side_effects=True, vmem_limit_bytes=40 * 1024 * 1024
        ),
        cost_estimate=pl.CostEstimate(
            flops=2 * STEPS * rows * block * cols,
            bytes_accessed=2 * (rows * block + held * cols + rows * cols),
            transcendentals=0,
        ),
        name="corner_product",
    )(upper_tiles, lower_tiles, upper, lower)


def solution(mesh):
    spec = P("col", "row")
    return jax.shard_map(body, mesh=mesh, in_specs=(spec,) * 4, out_specs=spec, check_vma=False)
```

time: 216 us -> 144 us (0.67)
  the two profiles are of different devices: /device:TPU:14 before, /device:TPU:7 now
where the time goes in v1:
time: 144 us
  Pallas kernels  138 us (96%)
  local copies, waits for them, and re-layouts  5.6 us (4%)
    pallas_call x1, Pallas kernels, body(): pl.pallas_call(run, out_shape=jax.ShapeDtypeStruct((rows, cols), jnp.bflo...  138 us
    unnamed x8, local copies, waits for them, and re-layouts  5.6 us

profile of v1, /device:TPU:7, one launch (start us, length us, event | category | flops | bytes accessed | tf_op | source)
XLA Modules:
  0.0 143.9 jit_solution(8466303904294728268)
XLA Ops:
  0.0 0.8 copy.5.refs_1_
  0.8 0.0 copy-start
  0.8 1.6 %copy-done = bf16[1024,1024]{1,0:T(8,128)(2,1)S(1)} copy-done((bf16[1024,1024]{1,0:T(8,128)(2,1)S(1)}, bf16[1024,1024]{1,0:T(8,128)(2,1)}, u32[]{:S(2)}) %copy-start) | copy-done | bytes 2097176
  2.4 0.0 copy-start.1
  2.4 1.6 %copy-done.1 = bf16[2048,512]{1,0:T(8,128)(2,1)S(1)} copy-done((bf16[2048,512]{1,0:T(8,128)(2,1)S(1)}, bf16[2048,512]{1,0:T(8,128)(2,1)}, u32[]{:S(2)}) %copy-start.1) | copy-done | bytes 2097176
  3.9 0.0 copy-start.2
  3.9 0.7 copy-done.2
  4.6 138.3 %corner_product.1 = bf16[1024,512]{1,0:T(8,128)(2,1)S(1)} custom-call(s32[8,8]{1,0:T(8,128)S(1)} %copy-done.2, s32[16,4]{1,0:T(8,128)S(1)} %copy.5.refs_1_, bf16[1024,1024]{1,0:T(8,128)(2,1)S(1)} %copy-done, bf16[2048,512]{1,0:T(8,128)(2,1)S(1)} %copy-done.1), custom_call_target="tpu_custom_call" | custom-call | flops 4294967296 | bytes 5242880 | tf_op jit(solution)/shard_map/corner_product/pallas_call | solution.py:218
  143.0 1.0 copy.7
Async XLA Ops:
  0.8 1.6 %copy-start = (bf16[1024,1024]{1,0:T(8,128)(2,1)S(1)}, bf16[1024,1024]{1,0:T(8,128)(2,1)}, u32[]{:S(2)}) copy-start(bf16[1024,1024]{1,0:T(8,128)(2,1)} %refs_2_.1) | copy-start | bytes 6291460
  2.4 1.6 %copy-start.1 = (bf16[2048,512]{1,0:T(8,128)(2,1)S(1)}, bf16[2048,512]{1,0:T(8,128)(2,1)}, u32[]{:S(2)}) copy-start(bf16[2048,512]{1,0:T(8,128)(2,1)} %refs_3_.1) | copy-start | bytes 6291460
  3.9 0.7 copy-start.2

commit v2 on v1

v2 whole, which is shorter than its diff:
```python
import jax
import jax.numpy as jnp
from jax import lax
from jax.experimental import pallas as pl
from jax.experimental.pallas import tpu as pltpu
from jax.sharding import PartitionSpec as P

STEPS = 4
TILE = 128
X = 4
SUB = 1
BEGIN = 3
LATE = 3
PIECES = 4
ORDER = (1, 2, 3, 0)
PARTS = 4
MESH = pl.DeviceIdType.MESH


def kernel(
    n_row, n_col, upper_tiles_in, lower_tiles_in, upper, lower, out,
    upper_tiles, lower_tiles, tile_load, ublocks, lblocks, relay,
    uload, lload, near_send, near_recv, far_send, far_recv, pair_send, pair_recv,
    low_send, low_recv, hop_send, hop_recv, goal_recv,
):
    r, c = lax.axis_index("row"), lax.axis_index("col")
    core, x = r % 2, c % X
    even = core == 0
    rows = TILE
    chunks = upper.shape[0] // rows
    held = lower.shape[0]
    quarter = held // PARTS

    def dev(dr, dc):
        return (lax.rem(r + dr + n_row, n_row), lax.rem(c + dc + n_col, n_col))

    first = x == 0
    last = x == X - 1
    origin_c = c - x
    goal = (r, lax.rem(origin_c + n_col - 1, n_col))

    barrier = pltpu.get_barrier_semaphore()

    def greet(device):
        pl.semaphore_signal(barrier, inc=1, device_id=device, device_id_type=MESH)

    tile_loads = (
        pltpu.make_async_copy(lower_tiles_in, lower_tiles, tile_load.at[0]),
        pltpu.make_async_copy(upper_tiles_in, upper_tiles, tile_load.at[1]),
    )
    for load in tile_loads:
        load.start()
    def load_upper(i):
        part = pl.ds(pl.multiple_of(i * rows, rows), rows)
        return pltpu.make_async_copy(upper.at[part], ublocks.at[0, part], uload.at[i])

    def load_lower(j):
        part = pl.ds(j * quarter, quarter)
        return pltpu.make_async_copy(lower.at[part], lblocks.at[part], lload.at[j])

    for i in range(BEGIN):
        load_upper(i).start()
    for j in ORDER:
        load_lower(j).start()
    for i in range(BEGIN, chunks):
        load_upper(i).start()

    greet(dev(2, 0))
    greet(dev(jnp.where(even, 1, 3), 0))
    greet(dev(jnp.where(even, 1, -1), 0))

    @pl.when(jnp.logical_not(last))
    def _():
        greet(dev(0, 1))

    @pl.when(last)
    def _():
        for j in range(PARTS):
            greet((r, lax.rem(origin_c + X + j, n_col)))

    @pl.when(jnp.logical_not(first))
    def _():
        greet((r, origin_c))

    pl.semaphore_wait(barrier, jnp.where(first, 3 + 1 + 3, 3 + 1 + 1))

    fine = rows // SUB
    nears = chunks * SUB

    def near(i):
        part = pl.ds(pl.multiple_of(i * fine, fine), fine)
        return pltpu.make_async_remote_copy(
            ublocks.at[0, part], ublocks.at[2, part], near_send.at[i], near_recv.at[i],
            device_id=dev(-2, 0), device_id_type=MESH,
        )

    def far(i):
        part = pl.ds(pl.multiple_of(i * rows, rows), rows)
        return pltpu.make_async_remote_copy(
            ublocks.at[0, part], ublocks.at[jnp.where(even, 3, 1), part], far_send.at[i], far_recv.at[i],
            device_id=dev(jnp.where(even, -3, -1), 0), device_id_type=MESH,
        )

    def pair(i):
        part = pl.ds(pl.multiple_of(i * fine, fine), fine)
        return pltpu.make_async_remote_copy(
            ublocks.at[2, part], ublocks.at[jnp.where(even, 1, 3), part], pair_send.at[i], pair_recv.at[i],
            device_id=dev(jnp.where(even, 1, -1), 0), device_id_type=MESH,
        )

    def low(j):
        return pltpu.make_async_remote_copy(
            lblocks.at[pl.ds(j * quarter, quarter)], lblocks.at[pl.ds(held + j * quarter, quarter)],
            low_send.at[j], low_recv.at[j], device_id=dev(0, -1), device_id_type=MESH,
        )

    piece = quarter // PIECES

    def hop(j, h):
        return pltpu.make_async_remote_copy(
            lblocks.at[pl.ds(j * quarter + h * piece, piece)], relay.at[pl.ds(h * piece, piece)],
            hop_send.at[j, h], hop_recv.at[h],
            device_id=(r, lax.rem(origin_c + j, n_col)), device_id_type=MESH,
        )

    def goal_first(h):
        return pltpu.make_async_remote_copy(
            lblocks.at[pl.ds(h * piece, piece)], lblocks.at[pl.ds(held + h * piece, piece)],
            hop_send.at[0, h], goal_recv.at[0, h], device_id=goal, device_id_type=MESH,
        )

    def goal_relay(h):
        return pltpu.make_async_remote_copy(
            relay.at[pl.ds(h * piece, piece)],
            lblocks.at[pl.ds(pl.multiple_of(held + x * quarter + h * piece, piece), piece)],
            hop_send.at[0, h], goal_recv.at[x, h], device_id=goal, device_id_type=MESH,
        )

    def goal_wait(j, h):
        return pltpu.make_async_remote_copy(
            relay.at[pl.ds(h * piece, piece)],
            lblocks.at[pl.ds(held + j * quarter + h * piece, piece)],
            hop_send.at[0, h], goal_recv.at[j, h], device_id=goal, device_id_type=MESH,
        )

    def mask_upper(i):
        part = pl.ds(pl.multiple_of(i * rows, rows), rows)
        for k in range(upper.shape[1] // TILE):
            at = (0, part, pl.ds(k * TILE, TILE))
            keep = upper_tiles[i, k].astype(jnp.float32)
            ublocks[at] = ublocks[at] * jnp.full((rows, TILE), keep, jnp.float32).astype(jnp.bfloat16)

    def mask_lower(i):
        part = pl.ds(pl.multiple_of(i * TILE, TILE), TILE)
        for k in range(lower.shape[1] // TILE):
            at = (part, pl.ds(k * TILE, TILE))
            keep = lower_tiles[k, i].astype(jnp.float32)
            lblocks[at] = lblocks[at] * jnp.full((TILE, TILE), keep, jnp.float32).astype(jnp.bfloat16)

    for load in tile_loads:
        load.wait()

    def begin_near():
        @pl.loop(0, BEGIN)
        def _(i):
            load_upper(i).wait()
            mask_upper(i)
            for n in range(SUB):
                near(i * SUB + n).start()

    @pl.when(jnp.logical_not(first))
    def _():
        begin_near()

    for j in ORDER:
        load_lower(j).wait()

        @pl.loop(0, quarter // TILE)
        def _(h):
            mask_lower(j * (quarter // TILE) + h)

        @pl.when(first)
        def _():
            for h in range(PIECES):
                if j == 0:
                    goal_first(h).start()
                else:
                    hop(j, h).start()

    @pl.when(first)
    def _():
        begin_near()

    @pl.loop(0, BEGIN)
    def _(i):
        far(i).start()

    @pl.loop(BEGIN, chunks)
    def _(i):
        load_upper(i).wait()
        mask_upper(i)
        far(i).start()

    @pl.when(jnp.logical_not(first))
    def _():
        for h in range(PIECES):
            hop(1, h).wait_recv()
            goal_relay(h).start()
        for j in range(PARTS):
            low(j).start()

    @pl.loop(BEGIN * SUB, nears)
    def _(i):
        near(i).start()

    def multiply(i):
        part = pl.ds(pl.multiple_of(i * rows, rows), rows)
        block = ublocks.shape[2]
        total = jnp.zeros((rows, lower.shape[1]), jnp.float32)
        for s in range(STEPS):
            total += jnp.dot(
                ublocks[s, part], lblocks[pl.ds(s * block, block)], preferred_element_type=jnp.float32
            )
        out[part] = total.astype(jnp.bfloat16)

    def step(i):
        near(i).wait_recv()
        pair(i).start()

    def finish(i):
        for n in range(SUB):
            pair(i * SUB + n).wait_recv()
        far(i).wait_recv()
        multiply(i)

    late = nears - LATE

    @pl.loop(0, late)
    def _(i):
        step(i)

    @pl.when(jnp.logical_not(last))
    def _():
        for j in range(PARTS):
            low(j).wait_recv()

    @pl.when(last)
    def _():
        for j in range(PARTS):
            for h in range(PIECES):
                goal_wait(j, h).wait_recv()

    @pl.loop(late, nears)
    def _(i):
        step(i)

        @pl.loop((i - late) * (chunks - 1) // LATE, (i + 1 - late) * (chunks - 1) // LATE)
        def _(n):
            finish(n)

    finish(chunks - 1)

    @pl.loop(0, nears)
    def _(i):
        near(i).wait_send()
        pair(i).wait_send()

    @pl.loop(0, chunks)
    def _(i):
        far(i).wait_send()

    @pl.when(first)
    def _():
        for h in range(PIECES):
            for j in range(1, PARTS):
                hop(j, h).wait_send()
            goal_first(h).wait_send()

    @pl.when(jnp.logical_not(first))
    def _():
        for j in range(PARTS):
            low(j).wait_send()
        for h in range(PIECES):
            goal_relay(h).wait_send()


def body(upper, lower, upper_tiles, lower_tiles):
    n_row, n_col = lax.axis_size("row"), lax.axis_size("col")
    rows, block = upper.shape
    held, cols = lower.shape
    chunks = rows // TILE
    dma = pltpu.SemaphoreType.DMA

    def run(*refs):
        kernel(n_row, n_col, *refs)

    return pl.pallas_call(
        run,
        out_shape=pltpu.VMEM((rows, cols), jnp.bfloat16),
        in_specs=[pl.BlockSpec(memory_space=pltpu.HBM)] * 4,
        out_specs=pl.BlockSpec(memory_space=pltpu.VMEM),
        scratch_shapes=[
            pltpu.SMEM(upper_tiles.shape, jnp.int32),
            pltpu.SMEM(lower_tiles.shape[::-1], jnp.int32),
            dma((2,)),
            pltpu.VMEM((STEPS, rows, block), jnp.bfloat16),
            pltpu.VMEM((2 * held, cols), jnp.bfloat16),
            pltpu.VMEM((held // PARTS, cols), jnp.bfloat16),
            dma((chunks,)), dma((PARTS,)),
            dma((chunks * SUB,)), dma((chunks * SUB,)),
            dma((chunks,)), dma((chunks,)),
            dma((chunks * SUB,)), dma((chunks * SUB,)),
            dma((PARTS,)), dma((PARTS,)),
            dma((PARTS, PIECES)), dma((PIECES,)), dma((PARTS, PIECES)),
        ],
        compiler_params=pltpu.CompilerParams(
            collective_id=0, has_side_effects=True, vmem_limit_bytes=40 * 1024 * 1024
        ),
        cost_estimate=pl.CostEstimate(
            flops=2 * STEPS * rows * block * cols,
            bytes_accessed=2 * (rows * block + held * cols + rows * cols),
            transcendentals=0,
        ),
        name="corner_product",
    )(*(pltpu.with_memory_space_constraint(a, pltpu.HBM) for a in (upper_tiles, lower_tiles.T, upper, lower)))


def solution(mesh):
    spec = P("col", "row")
    return jax.shard_map(body, mesh=mesh, in_specs=(spec,) * 4, out_specs=spec, check_vma=False)
```

time: 144 us -> 119 us (0.83); the launches traced: 144 us -> 117 us
  Pallas kernels: 138 us -> 116 us
  local copies, waits for them, and re-layouts: 5.6 us -> 0.97 us
    pallas_call x1, Pallas kernels: 138 us -> 116 us  [body(): pl.pallas_call(run, out_shape=pltpu.VMEM((rows, cols), jnp.bfloat16), in_...]
    unnamed x8 -> x1, local copies, waits for them, and re-layouts: 5.6 us -> 0.97 us
where the time goes in v2:
time: 119 us; the launch traced here: 117 us
  Pallas kernels  116 us (97%)
    pallas_call x1, Pallas kernels, body(): pl.pallas_call(run, out_shape=pltpu.VMEM((rows, cols), jnp.bfloat16), in_...  116 us

profile of v2, /device:TPU:7, one launch (start us, length us, event | category | flops | bytes accessed | tf_op | source)
XLA Modules:
  0.0 117.2 jit_solution(8128121591716147388)
XLA Ops:
  0.0 116.3 %corner_product.1 = bf16[1024,512]{1,0:T(8,128)(2,1)S(1)} custom-call(s32[8,8]{1,0:T(8,128)} %refs_0_.1, s32[4,16]{1,0:T(4,128)} %bitcast.1, bf16[1024,1024]{1,0:T(8,128)(2,1)} %refs_2_.1, bf16[2048,512]{1,0:T(8,128)(2,1)} %refs_3_.1), custom_call_target="tpu_custom_call" | custom-call | flops 4294967296 | bytes 5242880 | tf_op jit(solution)/shard_map/corner_product/pallas_call | solution.py:297
  116.3 1.0 copy.6

commit v3 on v2

--- a/solution.py
+++ b/solution.py
@@ -8,7 +8,6 @@
 STEPS = 4
 TILE = 128
 X = 4
-SUB = 1
 BEGIN = 3
 LATE = 3
 PIECES = 4
@@ -19,9 +18,9 @@
 
 def kernel(
     n_row, n_col, upper_tiles_in, lower_tiles_in, upper, lower, out,
-    upper_tiles, lower_tiles, tile_load, ublocks, lblocks, relay,
+    upper_tiles, lower_tiles, tile_load, ublocks, lblocks, relay, passed,
     uload, lload, near_send, near_recv, far_send, far_recv, pair_send, pair_recv,
-    low_send, low_recv, hop_send, hop_recv, goal_recv,
+    low_send, low_recv, hop_send, hop_recv, pass_recv, goal_send, goal_recv,
 ):
     r, c = lax.axis_index("row"), lax.axis_index("col")
     core, x = r % 2, c % X
@@ -37,12 +36,31 @@
     first = x == 0
     last = x == X - 1
     origin_c = c - x
-    goal = (r, lax.rem(origin_c + n_col - 1, n_col))
+    goal = (r, origin_c + X - 1)
 
     barrier = pltpu.get_barrier_semaphore()
 
     def greet(device):
         pl.semaphore_signal(barrier, inc=1, device_id=device, device_id_type=MESH)
+
+    greet(dev(2, 0))
+    greet(dev(jnp.where(even, 1, 3), 0))
+    greet(dev(jnp.where(even, 1, -1), 0))
+
+    @pl.when(jnp.logical_not(last))
+    def _():
+        greet(dev(0, 1))
+
+    @pl.when(last)
+    def _():
+        for j in range(PARTS - 1):
+            greet((r, origin_c + j))
+
+    greet(dev(0, X))
+
+    @pl.when(jnp.logical_not(first))
+    def _():
+        greet((r, origin_c))
 
     tile_loads = (
         pltpu.make_async_copy(lower_tiles_in, lower_tiles, tile_load.at[0]),
@@ -65,30 +83,8 @@
     for i in range(BEGIN, chunks):
         load_upper(i).start()
 
-    greet(dev(2, 0))
-    greet(dev(jnp.where(even, 1, 3), 0))
-    greet(dev(jnp.where(even, 1, -1), 0))
-
-    @pl.when(jnp.logical_not(last))
-    def _():
-        greet(dev(0, 1))
-
-    @pl.when(last)
-    def _():
-        for j in range(PARTS):
-            greet((r, lax.rem(origin_c + X + j, n_col)))
-
-    @pl.when(jnp.logical_not(first))
-    def _():
-        greet((r, origin_c))
-
-    pl.semaphore_wait(barrier, jnp.where(first, 3 + 1 + 3, 3 + 1 + 1))
-
-    fine = rows // SUB
-    nears = chunks * SUB
-
     def near(i):
-        part = pl.ds(pl.multiple_of(i * fine, fine), fine)
+        part = pl.ds(pl.multiple_of(i * rows, rows), rows)
         return pltpu.make_async_remote_copy(
             ublocks.at[0, part], ublocks.at[2, part], near_send.at[i], near_recv.at[i],
             device_id=dev(-2, 0), device_id_type=MESH,
@@ -102,7 +98,7 @@
         )
 
     def pair(i):
-        part = pl.ds(pl.multiple_of(i * fine, fine), fine)
+        part = pl.ds(pl.multiple_of(i * rows, rows), rows)
         return pltpu.make_async_remote_copy(
             ublocks.at[2, part], ublocks.at[jnp.where(even, 1, 3), part], pair_send.at[i], pair_recv.at[i],
             device_id=dev(jnp.where(even, 1, -1), 0), device_id_type=MESH,
@@ -123,24 +119,32 @@
             device_id=(r, lax.rem(origin_c + j, n_col)), device_id_type=MESH,
         )
 
-    def goal_first(h):
-        return pltpu.make_async_remote_copy(
-            lblocks.at[pl.ds(h * piece, piece)], lblocks.at[pl.ds(held + h * piece, piece)],
-            hop_send.at[0, h], goal_recv.at[0, h], device_id=goal, device_id_type=MESH,
-        )
-
-    def goal_relay(h):
-        return pltpu.make_async_remote_copy(
-            relay.at[pl.ds(h * piece, piece)],
-            lblocks.at[pl.ds(pl.multiple_of(held + x * quarter + h * piece, piece), piece)],
-            hop_send.at[0, h], goal_recv.at[x, h], device_id=goal, device_id_type=MESH,
-        )
-
-    def goal_wait(j, h):
-        return pltpu.make_async_remote_copy(
-            relay.at[pl.ds(h * piece, piece)],
-            lblocks.at[pl.ds(held + j * quarter + h * piece, piece)],
-            hop_send.at[0, h], goal_recv.at[j, h], device_id=goal, device_id_type=MESH,
+    def passing(source, target, sem, h):
+        return pltpu.make_async_remote_copy(
+            source.at[pl.ds(h * piece, piece)], target.at[pl.ds(h * piece, piece)],
+            hop_send.at[0, h], sem.at[h], device_id=dev(0, -X), device_id_type=MESH,
+        )
+
+    def arrived(j):
+        return lblocks.at[pl.ds(pl.multiple_of(held + j * quarter, quarter), quarter)]
+
+    def pass_on(h):
+        @pl.when(first)
+        def _():
+            passing(lblocks.at[pl.ds(0, quarter)], passed, pass_recv, h).start()
+
+        @pl.when(jnp.logical_not(jnp.logical_or(first, last)))
+        def _():
+            passing(relay, passed, pass_recv, h).start()
+
+        @pl.when(last)
+        def _():
+            passing(relay, arrived(PARTS - 1), goal_recv.at[PARTS - 1], h).start()
+
+    def to_goal(j, h):
+        return pltpu.make_async_remote_copy(
+            passed.at[pl.ds(h * piece, piece)], arrived(j).at[pl.ds(h * piece, piece)],
+            goal_send.at[h], goal_recv.at[j, h], device_id=goal, device_id_type=MESH,
         )
 
     def mask_upper(i):
@@ -160,17 +164,10 @@
     for load in tile_loads:
         load.wait()
 
-    def begin_near():
-        @pl.loop(0, BEGIN)
-        def _(i):
-            load_upper(i).wait()
-            mask_upper(i)
-            for n in range(SUB):
-                near(i * SUB + n).start()
-
-    @pl.when(jnp.logical_not(first))
-    def _():
-        begin_near()
+    @pl.loop(0, BEGIN)
+    def _(i):
+        load_upper(i).wait()
+        mask_upper(i)
 
     for j in ORDER:
         load_lower(j).wait()
@@ -179,17 +176,22 @@
         def _(h):
             mask_lower(j * (quarter // TILE) + h)
 
-        @pl.when(first)
-        def _():
+    pl.semaphore_wait(barrier, 4 + jnp.where(first, 3, 1) + jnp.where(last, 0, 1))
+
+    @pl.loop(0, BEGIN)
+    def _(i):
+        near(i).start()
+
+    @pl.when(first)
+    def _():
+        for j in range(1, PARTS):
             for h in range(PIECES):
-                if j == 0:
-                    goal_first(h).start()
-                else:
-                    hop(j, h).start()
-
-    @pl.when(first)
-    def _():
-        begin_near()
+                hop(j, h).start()
+
+    @pl.when(jnp.logical_not(first))
+    def _():
+        for j in range(PARTS):
+            low(j).start()
 
     @pl.loop(0, BEGIN)
     def _(i):
@@ -201,17 +203,22 @@
         mask_upper(i)
         far(i).start()
 
-    @pl.when(jnp.logical_not(first))
+    for h in range(PIECES):
+        @pl.when(jnp.logical_not(first))
+        def _():
+            hop(1, h).wait_recv()
+
+        pass_on(h)
+
+    @pl.loop(BEGIN, chunks)
+    def _(i):
+        near(i).start()
+
+    @pl.when(jnp.logical_not(last))
     def _():
         for h in range(PIECES):
-            hop(1, h).wait_recv()
-            goal_relay(h).start()
-        for j in range(PARTS):
-            low(j).start()
-
-    @pl.loop(BEGIN * SUB, nears)
-    def _(i):
-        near(i).start()
+            passing(relay, passed, pass_recv, h).wait_recv()
+            to_goal(x, h).start()
 
     def multiply(i):
         part = pl.ds(pl.multiple_of(i * rows, rows), rows)
@@ -228,12 +235,11 @@
         pair(i).start()
 
     def finish(i):
-        for n in range(SUB):
-            pair(i * SUB + n).wait_recv()
+        pair(i).wait_recv()
         far(i).wait_recv()
         multiply(i)
 
-    late = nears - LATE
+    late = chunks - LATE
 
     @pl.loop(0, late)
     def _(i):
@@ -248,40 +254,47 @@
     def _():
         for j in range(PARTS):
             for h in range(PIECES):
-                goal_wait(j, h).wait_recv()
-
-    @pl.loop(late, nears)
-    def _(i):
+                to_goal(j, h).wait_recv()
+
+    @pl.loop(0, late - 1)
+    def _(i):
+        finish(i)
+
+    @pl.loop(late, chunks)
+    def _(i):
+        finish(i - 1)
         step(i)
 
-        @pl.loop((i - late) * (chunks - 1) // LATE, (i + 1 - late) * (chunks - 1) // LATE)
-        def _(n):
-            finish(n)
-
-    finish(chunks - 1)
-
-    @pl.loop(0, nears)
+    @pl.loop(0, chunks - 1)
     def _(i):
         near(i).wait_send()
         pair(i).wait_send()
-
-    @pl.loop(0, chunks)
-    def _(i):
         far(i).wait_send()
+
+    far(chunks - 1).wait_send()
 
     @pl.when(first)
     def _():
         for h in range(PIECES):
             for j in range(1, PARTS):
                 hop(j, h).wait_send()
-            goal_first(h).wait_send()
 
     @pl.when(jnp.logical_not(first))
     def _():
         for j in range(PARTS):
             low(j).wait_send()
+
+    for h in range(PIECES):
+        passing(relay, passed, pass_recv, h).wait_send()
+
+    @pl.when(jnp.logical_not(last))
+    def _():
         for h in range(PIECES):
-            goal_relay(h).wait_send()
+            to_goal(x, h).wait_send()
+
+    finish(chunks - 1)
+    near(chunks - 1).wait_send()
+    pair(chunks - 1).wait_send()
 
 
 def body(upper, lower, upper_tiles, lower_tiles):
@@ -306,12 +319,13 @@
             pltpu.VMEM((STEPS, rows, block), jnp.bfloat16),
             pltpu.VMEM((2 * held, cols), jnp.bfloat16),
             pltpu.VMEM((held // PARTS, cols), jnp.bfloat16),
+            pltpu.VMEM((held // PARTS, cols), jnp.bfloat16),
             dma((chunks,)), dma((PARTS,)),
-            dma((chunks * SUB,)), dma((chunks * SUB,)),
             dma((chunks,)), dma((chunks,)),
-            dma((chunks * SUB,)), dma((chunks * SUB,)),
+            dma((chunks,)), dma((chunks,)),
+            dma((chunks,)), dma((chunks,)),
             dma((PARTS,)), dma((PARTS,)),
-            dma((PARTS, PIECES)), dma((PIECES,)), dma((PARTS, PIECES)),
+            dma((PARTS, PIECES)), dma((PIECES,)), dma((PIECES,)), dma((PIECES,)), dma((PARTS, PIECES)),
         ],
         compiler_params=pltpu.CompilerParams(
             collective_id=0, has_side_effects=True, vmem_limit_bytes=40 * 1024 * 1024

time: 119 us -> 117 us (0.983); the launches traced: 117 us -> 116 us
  no operation moved by 1% of the time
where the time goes in v3:
time: 117 us; the launch traced here: 116 us
  Pallas kernels  116 us (99%)
    pallas_call x1, Pallas kernels, body(): pl.pallas_call(run, out_shape=pltpu.VMEM((rows, cols), jnp.bfloat16), in_...  116 us

profile of v3, /device:TPU:7, one launch (start us, length us, event | category | flops | bytes accessed | tf_op | source)
XLA Modules:
  0.0 116.5 jit_solution(4359896544524255116)
XLA Ops:
  0.0 115.5 %corner_product.1 = bf16[1024,512]{1,0:T(8,128)(2,1)S(1)} custom-call(s32[8,8]{1,0:T(8,128)} %refs_0_.1, s32[4,16]{1,0:T(4,128)} %bitcast.1, bf16[1024,1024]{1,0:T(8,128)(2,1)} %refs_2_.1, bf16[2048,512]{1,0:T(8,128)(2,1)} %refs_3_.1), custom_call_target="tpu_custom_call" | custom-call | flops 4294967296 | bytes 5242880 | tf_op jit(solution)/shard_map/corner_product/pallas_call | solution.py:310
  115.5 1.0 copy.6

commit v4 on v3

--- a/solution.py
+++ b/solution.py
@@ -10,7 +10,8 @@
 X = 4
 BEGIN = 3
 LATE = 3
-PIECES = 4
+FARS = 2
+PIECES = 1
 ORDER = (1, 2, 3, 0)
 PARTS = 4
 MESH = pl.DeviceIdType.MESH
@@ -90,8 +91,10 @@
             device_id=dev(-2, 0), device_id_type=MESH,
         )
 
+    far_rows = upper.shape[0] // FARS
+
     def far(i):
-        part = pl.ds(pl.multiple_of(i * rows, rows), rows)
+        part = pl.ds(pl.multiple_of(i * far_rows, far_rows), far_rows)
         return pltpu.make_async_remote_copy(
             ublocks.at[0, part], ublocks.at[jnp.where(even, 3, 1), part], far_send.at[i], far_recv.at[i],
             device_id=dev(jnp.where(even, -3, -1), 0), device_id_type=MESH,
@@ -104,10 +107,10 @@
             device_id=dev(jnp.where(even, 1, -1), 0), device_id_type=MESH,
         )
 
-    def low(j):
-        return pltpu.make_async_remote_copy(
-            lblocks.at[pl.ds(j * quarter, quarter)], lblocks.at[pl.ds(held + j * quarter, quarter)],
-            low_send.at[j], low_recv.at[j], device_id=dev(0, -1), device_id_type=MESH,
+    def low():
+        return pltpu.make_async_remote_copy(
+            lblocks.at[pl.ds(0, held)], lblocks.at[pl.ds(held, held)], low_send, low_recv,
+            device_id=dev(0, -1), device_id_type=MESH,
         )
 
     piece = quarter // PIECES
@@ -190,18 +193,16 @@
 
     @pl.when(jnp.logical_not(first))
     def _():
-        for j in range(PARTS):
-            low(j).start()
-
-    @pl.loop(0, BEGIN)
-    def _(i):
-        far(i).start()
+        low().start()
 
     @pl.loop(BEGIN, chunks)
     def _(i):
         load_upper(i).wait()
         mask_upper(i)
-        far(i).start()
+
+        @pl.when((i + 1) % (chunks // FARS) == 0)
+        def _():
+            far(i // (chunks // FARS)).start()
 
     for h in range(PIECES):
         @pl.when(jnp.logical_not(first))
@@ -236,7 +237,11 @@
 
     def finish(i):
         pair(i).wait_recv()
-        far(i).wait_recv()
+
+        @pl.when(i % (chunks // FARS) == 0)
+        def _():
+            far(i // (chunks // FARS)).wait_recv()
+
         multiply(i)
 
     late = chunks - LATE
@@ -247,8 +252,7 @@
 
     @pl.when(jnp.logical_not(last))
     def _():
-        for j in range(PARTS):
-            low(j).wait_recv()
+        low().wait_recv()
 
     @pl.when(last)
     def _():
@@ -269,9 +273,9 @@
     def _(i):
         near(i).wait_send()
         pair(i).wait_send()
+
+    for i in range(FARS):
         far(i).wait_send()
-
-    far(chunks - 1).wait_send()
 
     @pl.when(first)
     def _():
@@ -281,8 +285,7 @@
 
     @pl.when(jnp.logical_not(first))
     def _():
-        for j in range(PARTS):
-            low(j).wait_send()
+        low().wait_send()
 
     for h in range(PIECES):
         passing(relay, passed, pass_recv, h).wait_send()
@@ -322,9 +325,9 @@
             pltpu.VMEM((held // PARTS, cols), jnp.bfloat16),
             dma((chunks,)), dma((PARTS,)),
             dma((chunks,)), dma((chunks,)),
+            dma((FARS,)), dma((FARS,)),
             dma((chunks,)), dma((chunks,)),
-            dma((chunks,)), dma((chunks,)),
-            dma((PARTS,)), dma((PARTS,)),
+            dma, dma,
             dma((PARTS, PIECES)), dma((PIECES,)), dma((PIECES,)), dma((PIECES,)), dma((PARTS, PIECES)),
         ],
         compiler_params=pltpu.CompilerParams(

time: 117 us -> 117 us (level)
  no operation moved by 1% of the time
where the time goes in v4:
time: 117 us; the launch traced here: 116 us
  Pallas kernels  115 us (98%)
    pallas_call x1, Pallas kernels, body(): pl.pallas_call(run, out_shape=pltpu.VMEM((rows, cols), jnp.bfloat16), in_...  115 us

profile of v4, /device:TPU:7, one launch (start us, length us, event | category | flops | bytes accessed | tf_op | source)
XLA Modules:
  0.0 116.0 jit_solution(13105301985870903713)
XLA Ops:
  0.0 115.0 %corner_product.1 = bf16[1024,512]{1,0:T(8,128)(2,1)S(1)} custom-call(s32[8,8]{1,0:T(8,128)} %refs_0_.1, s32[4,16]{1,0:T(4,128)} %bitcast.1, bf16[1024,1024]{1,0:T(8,128)(2,1)} %refs_2_.1, bf16[2048,512]{1,0:T(8,128)(2,1)} %refs_3_.1), custom_call_target="tpu_custom_call" | custom-call | flops 4294967296 | bytes 5242880 | tf_op jit(solution)/shard_map/corner_product/pallas_call | solution.py:313
  115.1 1.0 copy.6

commit v5 on v4

--- a/solution.py
+++ b/solution.py
@@ -10,7 +10,7 @@
 X = 4
 BEGIN = 3
 LATE = 3
-FARS = 2
+FARS = 1
 PIECES = 1
 ORDER = (1, 2, 3, 0)
 PARTS = 4

time: 117 us -> 117 us (level)
  no operation moved by 1% of the time
where the time goes in v5:
time: 117 us; the launch traced here: 116 us
  Pallas kernels  115 us (98%)
    pallas_call x1, Pallas kernels, body(): pl.pallas_call(run, out_shape=pltpu.VMEM((rows, cols), jnp.bfloat16), in_...  115 us

profile of v5, /device:TPU:7, one launch (start us, length us, event | category | flops | bytes accessed | tf_op | source)
XLA Modules:
  0.0 116.0 jit_solution(8813866143971557663)
XLA Ops:
  0.0 115.0 %corner_product.1 = bf16[1024,512]{1,0:T(8,128)(2,1)S(1)} custom-call(s32[8,8]{1,0:T(8,128)} %refs_0_.1, s32[4,16]{1,0:T(4,128)} %bitcast.1, bf16[1024,1024]{1,0:T(8,128)(2,1)} %refs_2_.1, bf16[2048,512]{1,0:T(8,128)(2,1)} %refs_3_.1), custom_call_target="tpu_custom_call" | custom-call | flops 4294967296 | bytes 5242880 | tf_op jit(solution)/shard_map/corner_product/pallas_call | solution.py:313
  115.0 1.0 copy.6
